TPU v7x, 32 devices: a whole 2x2x4 slice. The times are simulated.
32 devices in a mesh: fsdp: 8 (over y, x, core), ep: 4 (over z).
Axes of the slice: x: 2, y: 2, z: 4, core: 2. Of those that a mesh axis runs over, the one named last changes fastest.
Arguments:
- expert_ids: int32 [128, 4], P('ep'), may hold values from 0 to 15, all different within a row; in each aligned block of 32 rows (0 to 31, 32 to 63, ...) at most 16 rows name the same one
- route_weights: float32 [128, 4], P('ep'), may hold values from 0.1 to 1
- residual_grad: bfloat16 [128, 6144], P('ep', 'fsdp'), may hold values from -6 to 6
- hidden_grad: bfloat16 [32, 64, 2688], P('ep'), may hold values from -6 to 6
- gate_pre: bfloat16 [32, 64, 2688], P('ep'), may hold values from -6 to 6
- up_pre: bfloat16 [32, 64, 2688], P('ep'), may hold values from -6 to 6
- gate_weight: bfloat16 [32, 6144, 2688], P('ep', 'fsdp'), may hold values from -0.0625 to 0.0625
- up_weight: bfloat16 [32, 6144, 2688], P('ep', 'fsdp'), may hold values from -0.0625 to 0.0625
- attn_context: bfloat16 [2048, 6144], P('fsdp', 'ep'), may hold values from -6 to 6
- attn_grad: bfloat16 [2048, 6144], P('fsdp'), may hold values from -6 to 6
Outputs:
- input_grad: bfloat16 [128, 6144], P('ep', 'fsdp')
- proj_weight_grad: float32 [6144, 6144], P('ep', 'fsdp')
Inputs may be any that keep to these rules, and one draw needn't show every extreme that they name: `expert_ids`: each row names 4 different experts. Among the rows of one ep index no expert is named more than 16 times, a bound that some block reaches.
All inputs are finite; a program needn't handle non-finite values.
Results may differ from a plain program's by a relative error of at most 0.005.
Values may be sent and summed in bfloat16 or wider, within the bound.
A program may use at most 192 MiB of HBM per device.

v0:
```python
import jax
import jax.numpy as jnp
from jax import lax
from jax.sharding import PartitionSpec as P


def local_slots(expert_ids, experts):
    tokens, chosen = expert_ids.shape
    flat = expert_ids.reshape(tokens * chosen)
    onehot = (flat[:, None] == jnp.arange(experts, dtype=jnp.int32)[None, :]).astype(jnp.int32)
    before = jnp.cumsum(onehot, axis=0) - onehot
    return jnp.sum(before * onehot, axis=1).reshape(tokens, chosen)


def shards(
    expert_ids,
    route_weights,
    residual_grad,
    hidden_grad,
    gate_pre,
    up_pre,
    gate_weight,
    up_weight,
    attn_context,
    attn_grad,
):
    gate = gate_pre.astype(jnp.float32)
    upper = up_pre.astype(jnp.float32)
    grads = hidden_grad.astype(jnp.float32)
    sig = jax.nn.sigmoid(gate)
    up_term = (grads * gate * sig).astype(jnp.bfloat16)
    gate_term = (grads * upper * sig * (1.0 + gate * (1.0 - sig))).astype(jnp.bfloat16)
    rows_out = jnp.einsum(
        "brh,bdh->brd", gate_term, gate_weight, preferred_element_type=jnp.float32
    )
    rows_out = rows_out + jnp.einsum(
        "brh,bdh->brd", up_term, up_weight, preferred_element_type=jnp.float32
    )
    rows_out = rows_out.astype(jnp.bfloat16)
    received = lax.all_to_all(rows_out, "ep", split_axis=1, concat_axis=0, tiled=True)
    all_blocks, capacity, columns = received.shape
    received = received.reshape(all_blocks * capacity, columns).astype(jnp.float32)
    experts = all_blocks // 2
    slots = local_slots(expert_ids, experts)
    lower_col = 2 * expert_ids * capacity + slots
    upper_col = lower_col + capacity
    col_ids = jnp.arange(all_blocks * capacity, dtype=jnp.int32)[None, None, :]
    picks = (col_ids == lower_col[:, :, None]).astype(jnp.float32) + (
        col_ids == upper_col[:, :, None]
    ).astype(jnp.float32)
    combine = jnp.sum(route_weights[:, :, None] * picks, axis=1)
    gathered_sum = jnp.dot(combine, received, precision=lax.Precision.HIGHEST)
    input_grad = (residual_grad.astype(jnp.float32) + gathered_sum).astype(jnp.bfloat16)
    owned = lax.psum_scatter(
        jnp.einsum("tj,ti->ji", attn_grad, attn_context, preferred_element_type=jnp.float32),
        "fsdp",
        scatter_dimension=0,
        tiled=True,
    )
    proj_weight_grad = owned.T
    return (input_grad, proj_weight_grad)


def solution(mesh):
    return jax.shard_map(
        shards,
        mesh=mesh,
        in_specs=(
            P("ep", None),
            P("ep", None),
            P("ep", "fsdp"),
            P("ep", None, None),
            P("ep", None, None),
            P("ep", None, None),
            P("ep", "fsdp", None),
            P("ep", "fsdp", None),
            P("fsdp", "ep"),
            P("fsdp", None),
        ),
        out_specs=(P("ep", "fsdp"), P("ep", "fsdp")),
        check_vma=False,
    )
```

profile of v0, /device:TPU:0, one launch (start us, length us, event | category | flops | bytes accessed | tf_op | source)
XLA Modules:
  0.0 266.1 jit_solution(18189367980090005260)
XLA Ops:
  7.2 0.0 copy-start
  7.2 0.0 reduce-scatter.2.cloned.1.call-start
  7.2 1.8 copy-done
  9.1 15.9 %fusion.21 = f32[6144,1536]{1,0:T(8,128)} fusion(bf16[256,6144]{1,0:T(8,128)(2,1)S(1)} %copy-done, bf16[256,1536]{1,0:T(8,128)(2,1)} %param.18), kind=kOutput, calls=%fused_computation.30 | convolution fusion | flops 4831838208 | bytes 41680896 | tf_op jit(solution)/shard_map/tj,ti->ji/dot_general | solution.py:55
  24.9 0.0 copy-start.5
  24.9 0.0 reduce-scatter.2.cloned.1.call-update
  25.0 1.8 copy-done.5
  26.7 19.7 %fusion.9 = f32[8,64,768]{2,1,0:T(8,128)} fusion(bf16[8,768,2688]{2,1,0:T(8,128)(2,1)} %param.17, bf16[8,64,2688]{2,1,0:T(8,128)(2,1)S(1)} %copy-done.5, bf16[8,64,2688]{2,1,0:T(8,128)(2,1)} %param.13), kind=kOutput, calls=%fused_computation.13 | convolution fusion | flops 2124939264 | bytes 40108032 | tf_op jit(solution)/shard_map/brh,bdh->brd/dot_general | solution.py:36
  46.4 0.0 copy-start.3
  46.4 0.0 copy-start.4
  46.4 0.0 copy-start.2
  46.4 25.9 %add_convert_fusion = bf16[8,64,768]{2,1,0:T(8,128)(2,1)S(1)} fusion(f32[8,64,768]{2,1,0:T(8,128)} %fusion.9, bf16[8,768,2688]{2,1,0:T(8,128)(2,1)} %param.16, bf16[8,64,2688]{2,1,0:T(8,128)(2,1)} %param.13, bf16[8,64,2688]{2,1,0:T(8,128)(2,1)} %param.14, bf16[8,64,2688]{2,1,0:T(8,128)(2,1)} %param.15), kind=kOutput, calls=%fused_computation.17 | convolution fusion | flops 2132606976 | bytes 43646976 | tf_op jit(solution)/shard_map/brh,bdh->brd/dot_general | solution.py:33
  72.3 1.3 copy.48
  73.6 6.7 %all-to-all-start = ((bf16[8,64,768]{2,0,1:T(8,128)(2,1)}), bf16[8,64,768]{2,0,1:T(8,128)(2,1)}, u32[]{:S(2)}, u32[]{:S(2)}) async-start(bf16[8,64,768]{2,0,1:T(8,128)(2,1)} %copy.48), calls=%async_computation | async-start | bytes 1572864 | tf_op jit(solution)/shard_map/all_to_all | solution.py:40
  80.3 0.0 copy-done.3
  80.3 0.1 copy.46
  80.4 0.1 eq.42
  80.5 0.1 fusion.18
  80.6 0.2 reduce_window_sum.11
  80.8 0.2 select_reduce_fusion
  81.0 0.1 reshape.15
  81.1 0.1 copy.47
  81.2 0.0 copy-done.4
  81.2 0.1 multiply_reduce_fusion
  81.3 18.9 %all-to-all-done = bf16[8,64,768]{2,0,1:T(8,128)(2,1)} async-done(((bf16[8,64,768]{2,0,1:T(8,128)(2,1)}), bf16[8,64,768]{2,0,1:T(8,128)(2,1)}, u32[]{:S(2)}, u32[]{:S(2)}) %all-to-all-start) | async-done | bytes 786464 | tf_op jit(solution)/shard_map/all_to_all | solution.py:40
  100.2 0.0 copy-start.1
  100.2 1.4 copy.50
  101.6 0.0 copy-done.2
  101.6 1.1 fusion.17
  102.8 150.4 %reduce-scatter.2.cloned.1.call-done = f32[768,1536]{1,0:T(8,128)} async-done(((f32[6144,1536]{1,0:T(8,128)}), f32[768,1536]{1,0:T(8,128)}) %reduce-scatter.2.cloned.1.call-update) | async-done | bytes 4718608 | tf_op jit(solution)/shard_map/reduce_scatter | solution.py:54
  253.2 6.0 %copy.51 = f32[1536,768]{1,0:T(8,128)} copy(f32[1536,768]{0,1:T(8,128)} %bitcast.11) | data formatting | bytes 9437184
  259.2 0.0 copy-done.1
  (1 shorter events, 0.0 us)
Async XLA Ops:
  7.2 1.9 copy-start
  7.2 246.0 %reduce-scatter.2.cloned.1.call-start = ((), (), s32[]{:S(2)}) async-start(), calls=%async_computation.2 | async-start | bytes 42467328 | tf_op jit(solution)/shard_map/reduce_scatter | solution.py:54
  24.9 1.8 copy-start.5
  46.4 33.9 %copy-start.3 = (s32[32,4]{0,1:T(4,128)S(1)}, s32[32,4]{0,1:T(4,128)}, u32[]{:S(2)}) copy-start(s32[32,4]{0,1:T(4,128)} %param.10) | copy-start | bytes 1540
  46.4 34.8 %copy-start.4 = (f32[32,4]{0,1:T(4,128)S(1)}, f32[32,4]{0,1:T(4,128)}, u32[]{:S(2)}) copy-start(f32[32,4]{0,1:T(4,128)} %param.11) | copy-start | bytes 1540
  46.4 55.2 %copy-start.2 = (bf16[32,768]{1,0:T(8,128)(2,1)S(1)}, bf16[32,768]{1,0:T(8,128)(2,1)}, u32[]{:S(2)}) copy-start(bf16[32,768]{1,0:T(8,128)(2,1)} %param.12) | copy-start | bytes 147460
  73.6 26.6 %all-to-all-start = ((bf16[8,64,768]{2,0,1:T(8,128)(2,1)}), bf16[8,64,768]{2,0,1:T(8,128)(2,1)}, u32[]{:S(2)}, u32[]{:S(2)}) async-start(bf16[8,64,768]{2,0,1:T(8,128)(2,1)} %copy.48), calls=%async_computation | async-start | bytes 1572864 | tf_op jit(solution)/shard_map/all_to_all | solution.py:40
  100.2 159.0 %copy-start.1 = (bf16[256,6144]{1,0:T(8,128)(2,1)S(1)}, bf16[256,6144]{1,0:T(8,128)(2,1)}, u32[]{:S(2)}) copy-start(bf16[256,6144]{1,0:T(8,128)(2,1)} %param.19) | copy-start | bytes 9437188
Sparse Core Ops, SparseCore 0:
  25.1 228.0 reduce-scatter.1
where the time goes:
time: 266 us
  waiting for transfers between devices  169 us (64%)
  matrix products  62.5 us (23%)
  between operations  14.1 us (5%)
  local copies, waits for them, and re-layouts  12.8 us (5%)
  starting transfers between devices  6.78 us (3%)
    reduce_scatter x1, waiting for transfers between devices, shards(): lax.psum_scatter(jnp.einsum('tj,ti->ji', attn_grad, attn_context, preferr...  150 us
    dot_general x1, matrix products, shards(): jnp.einsum('brh,bdh->brd', gate_term, gate_weight, preferred_element_type...  25.9 us
    dot_general x1, matrix products, shards(): jnp.einsum('brh,bdh->brd', up_term, up_weight, preferred_element_type=jnp...  19.7 us
    all_to_all x1, waiting for transfers between devices, shards(): lax.all_to_all(rows_out, 'ep', split_axis=1, concat_axis=0, tiled=True)  18.9 us
    dot_general x1, matrix products, shards(): jnp.einsum('tj,ti->ji', attn_grad, attn_context, preferred_element_type=j...  15.9 us
    unnamed x14, local copies, waits for them, and re-layouts  9.74 us
    all_to_all x1, starting transfers between devices, shards(): lax.all_to_all(rows_out, 'ep', split_axis=1, concat_axis=0, tiled=True)  6.74 us
  transfers between devices with their start and end apart: 2, of which 2 were waited for; matrix products, arithmetic and copies ran while one was open for 19% of the time, Pallas kernels for 0%

commit v1 on v0

--- a/solution.py
+++ b/solution.py
@@ -1,7 +1,14 @@
+import functools
+
 import jax
 import jax.numpy as jnp
 from jax import lax
+from jax.experimental import pallas as pl
+from jax.experimental.pallas import tpu as pltpu
 from jax.sharding import PartitionSpec as P
+
+MESH = pl.DeviceIdType.MESH
+SLOT_COUNT = 3
 
 
 def local_slots(expert_ids, experts):
@@ -12,7 +19,7 @@
     return jnp.sum(before * onehot, axis=1).reshape(tokens, chosen)
 
 
-def shards(
+def general_shards(
     expert_ids,
     route_weights,
     residual_grad,
@@ -51,17 +58,435 @@
     combine = jnp.sum(route_weights[:, :, None] * picks, axis=1)
     gathered_sum = jnp.dot(combine, received, precision=lax.Precision.HIGHEST)
     input_grad = (residual_grad.astype(jnp.float32) + gathered_sum).astype(jnp.bfloat16)
-    owned = lax.psum_scatter(
-        jnp.einsum("tj,ti->ji", attn_grad, attn_context, preferred_element_type=jnp.float32),
-        "fsdp",
-        scatter_dimension=0,
-        tiled=True,
-    )
-    proj_weight_grad = owned.T
+    context_all = lax.all_gather(attn_context, "fsdp", axis=0, tiled=True)
+    grad_all = lax.all_to_all(attn_grad, "fsdp", split_axis=1, concat_axis=0, tiled=True)
+    proj_weight_grad = jnp.einsum(
+        "ti,tj->ij", context_all, grad_all, preferred_element_type=jnp.float32
+    )
     return (input_grad, proj_weight_grad)
 
 
+def kernel(
+    n_ep,
+    ids_ref,
+    route_ref,
+    residual_ref,
+    hidden_hbm,
+    gate_hbm,
+    up_hbm,
+    gate_weight_hbm,
+    up_weight_hbm,
+    context_hbm,
+    grad_hbm,
+    input_grad_ref,
+    proj_hbm,
+    hidden_buf,
+    gate_buf,
+    up_buf,
+    gate_weight_buf,
+    up_weight_buf,
+    gate_term,
+    up_term,
+    half_rows,
+    rows_out,
+    rows_in,
+    context_all,
+    grad_all,
+    total,
+    load_sem,
+    own_sem,
+    store_sem,
+    context_send,
+    context_recv,
+    grad_send,
+    grad_recv,
+    rows_send,
+    rows_recv,
+):
+    f32, bf16 = jnp.float32, jnp.bfloat16
+    blocks, slots, hidden = hidden_hbm.shape
+    columns = gate_weight_hbm.shape[1]
+    tokens, context_cols = context_hbm.shape
+    cap = slots // n_ep
+    quarter = tokens // n_ep
+    half = tokens // 2
+
+    f = lax.axis_index("fsdp")
+    z = lax.axis_index("ep")
+    core, x, y = f % 2, (f // 2) % 2, f // 4
+
+    def at(yy, xx, cc):
+        return yy * 4 + xx * 2 + cc
+
+    sib = at(y, x, 1 - core)
+    x_same, x_other = at(y, 1 - x, core), at(y, 1 - x, 1 - core)
+    y_same, y_other = at(1 - y, x, core), at(1 - y, x, 1 - core)
+    d_same, d_other = at(1 - y, 1 - x, core), at(1 - y, 1 - x, 1 - core)
+    own_chip, x_chip, y_chip, d_chip = f // 2, x_same // 2, y_same // 2, d_same // 2
+
+    sources = (gate_weight_hbm, up_weight_hbm, hidden_hbm, gate_hbm, up_hbm)
+    buffers = (gate_weight_buf, up_weight_buf, hidden_buf, gate_buf, up_buf)
+
+    def loads(block):
+        slot = block % SLOT_COUNT
+        return [
+            pltpu.make_async_copy(src.at[block], buf.at[slot], load_sem.at[i, slot])
+            for i, (src, buf) in enumerate(zip(sources, buffers))
+        ]
+
+    for block in range(SLOT_COUNT - 1):
+        for copy in loads(block):
+            copy.start()
+
+    def grad_columns(who):
+        return pl.ds(pl.multiple_of(who * columns, 128), columns)
+
+    own_copies = [
+        pltpu.make_async_copy(context_hbm, context_all.at[f], own_sem.at[0]),
+        pltpu.make_async_copy(grad_hbm.at[:, grad_columns(f)], grad_all.at[f], own_sem.at[1]),
+    ]
+    for copy in own_copies:
+        copy.start()
+
+    def remote(src, dst, send, recv, i, to):
+        return pltpu.make_async_remote_copy(
+            src_ref=src,
+            dst_ref=dst,
+            send_sem=send.at[i],
+            recv_sem=recv.at[i],
+            device_id=to,
+            device_id_type=MESH,
+        )
+
+    first, second = pl.ds(0, half), pl.ds(half, half)
+    context_moves = (
+        (context_hbm, context_all.at[f], sib),
+        (context_hbm, context_all.at[f], x_same),
+        (context_hbm, context_all.at[f], y_same),
+        (context_all.at[x_same, first], context_all.at[x_same, first], y_same),
+        (context_all.at[y_same, second], context_all.at[y_same, second], x_same),
+        (context_all.at[x_same], context_all.at[x_same], sib),
+        (context_all.at[y_same], context_all.at[y_same], sib),
+        (context_all.at[d_same, first], context_all.at[d_same, first], sib),
+        (context_all.at[d_same, second], context_all.at[d_same, second], sib),
+    )
+    context_lands = (
+        context_all.at[sib],
+        context_all.at[x_same],
+        context_all.at[y_same],
+        context_all.at[d_same, first],
+        context_all.at[d_same, second],
+        context_all.at[x_other],
+        context_all.at[y_other],
+        context_all.at[d_other, first],
+        context_all.at[d_other, second],
+    )
+
+    def context_out(i):
+        src, dst, to = context_moves[i]
+        return remote(src, dst, context_send, context_recv, i, (to, z))
+
+    def context_in(i):
+        land = context_lands[i]
+        return remote(land, land, context_send, context_recv, i, (context_moves[i][2], z))
+
+    def share(who):
+        return pl.ds(pl.multiple_of(who * quarter, quarter), quarter)
+
+    pair = pl.ds(2 * d_chip, 2)
+    grad_targets = (sib, x_same, x_other, y_same, y_other, d_same, d_other)
+
+    def grad_out(i):
+        if i < 5:
+            to = grad_targets[i]
+            src, dst = grad_hbm.at[:, grad_columns(to)], grad_all.at[f]
+        elif i < 7:
+            to = grad_targets[i]
+            src, dst = grad_hbm.at[share(z), grad_columns(to)], grad_all.at[f, share(z)]
+        else:
+            src = dst = grad_all.at[pair, share(z)]
+            return remote(src, dst, grad_send, grad_recv, i, (f, (z + i - 6) % n_ep))
+        return remote(src, dst, grad_send, grad_recv, i, (to, z))
+
+    def grad_in(i):
+        if i < 5:
+            land, to = grad_all.at[grad_targets[i]], (grad_targets[i], z)
+        elif i < 7:
+            land, to = grad_all.at[grad_targets[i], share(z)], (grad_targets[i], z)
+        else:
+            from_z = (z + n_ep - (i - 6)) % n_ep
+            land, to = grad_all.at[pair, share(from_z)], (f, from_z)
+        return remote(land, land, grad_send, grad_recv, i, to)
+
+    def rows_move(k):
+        to = (z + k) % n_ep
+        return remote(rows_out.at[to], rows_in.at[z], rows_send, rows_recv, k - 1, (f, to))
+
+    def rows_land(k):
+        source = (z + n_ep - k) % n_ep
+        land = rows_in.at[source]
+        return remote(land, land, rows_send, rows_recv, k - 1, (f, source))
+
+    barrier = pltpu.get_barrier_semaphore()
+    peers = [(who, z) for who in grad_targets] + [(f, (z + k) % n_ep) for k in range(1, n_ep)]
+    for who in peers:
+        pl.semaphore_signal(barrier, inc=1, device_id=who, device_id_type=MESH)
+    pl.semaphore_wait(barrier, len(peers))
+
+    for i in (1, 2, 0):
+        context_out(i).start()
+    for i in (5, 6, 0):
+        grad_out(i).start()
+
+    chunk = hidden // 7 if hidden % (7 * 128) == 0 else hidden
+
+    def expert_step(block, carry):
+        slot = block % SLOT_COUNT
+
+        @pl.when(block + (SLOT_COUNT - 1) < blocks)
+        def _():
+            for copy in loads(block + (SLOT_COUNT - 1)):
+                copy.start()
+
+        @pl.when(block == 2)
+        def _():
+            for i in (1, 3, 2, 4):
+                grad_out(i).start()
+
+        @pl.when(block == blocks - 2)
+        def _():
+            context_in(1).wait_recv()
+            context_out(3).start()
+            context_out(5).start()
+            context_in(2).wait_recv()
+            context_out(4).start()
+            context_out(6).start()
+            grad_in(5).wait_recv()
+            grad_in(6).wait_recv()
+            for i in (7, 8, 9):
+                grad_out(i).start()
+
+        for copy in loads(block):
+            copy.wait()
+        for start in range(0, hidden, chunk):
+            cols = pl.ds(start, chunk)
+            grads = hidden_buf[slot, :, cols].astype(f32)
+            gate = gate_buf[slot, :, cols].astype(f32)
+            upper = up_buf[slot, :, cols].astype(f32)
+            sig = 1.0 / (1.0 + jnp.exp(-gate))
+            scaled = grads * sig
+            up_term[:, cols] = (scaled * gate).astype(bf16)
+            gate_term[:, cols] = (scaled * upper * (1.0 + gate * (1.0 - sig))).astype(bf16)
+        dims = (((1,), (1,)), ((), ()))
+        part = lax.dot_general(
+            gate_term[...], gate_weight_buf[slot], dims, preferred_element_type=f32
+        )
+        part = part + lax.dot_general(
+            up_term[...], up_weight_buf[slot], dims, preferred_element_type=f32
+        )
+
+        @pl.when(block % 2 == 0)
+        def _():
+            half_rows[...] = part
+
+        @pl.when(block % 2 == 1)
+        def _():
+            both = (half_rows[...] + part).astype(bf16)
+            for dest in range(n_ep):
+                rows_out[dest, block // 2] = both[dest * cap : (dest + 1) * cap]
+
+        return carry
+
+    lax.fori_loop(0, blocks, expert_step, 0)
+
+    for k in range(1, n_ep):
+        rows_move(k).start()
+    rows_in[z] = rows_out[z]
+
+    step_cols = 256
+    steps = context_cols // step_cols
+
+    def store(i):
+        rows = pl.ds(pl.multiple_of(i * step_cols, step_cols), step_cols)
+        return pltpu.make_async_copy(total.at[rows], proj_hbm.at[rows], store_sem.at[i])
+
+    def chip_product(chip, begin, end):
+        def step(i, carry):
+            cols = pl.ds(pl.multiple_of(i * step_cols, step_cols), step_cols)
+            left = context_all[pl.ds(2 * chip, 2), :, cols].reshape(2 * tokens, step_cols)
+            right = grad_all[pl.ds(2 * chip, 2)].reshape(2 * tokens, columns)
+            product = lax.dot_general(
+                left, right, (((0,), (0,)), ((), ())), preferred_element_type=f32
+            )
+            if begin:
+                total[cols, :] = product
+            else:
+                total[cols, :] += product
+            if end:
+                store(i).start()
+            return carry
+
+        lax.fori_loop(0, steps, step, 0)
+
+    for copy in own_copies:
+        copy.wait()
+    context_in(0).wait_recv()
+    grad_in(0).wait_recv()
+    chip_product(own_chip, True, False)
+
+    routed, top = ids_ref.shape
+    width = n_ep * (blocks // 2) * cap
+    place = lax.broadcasted_iota(jnp.int32, (routed, width), 1)
+    expert, row = place // cap, place % cap
+    named = jnp.zeros((routed, width), f32)
+    weight = jnp.zeros((routed, width), f32)
+    for k in range(top):
+        match = ids_ref[:, k : k + 1] == expert
+        named = named + jnp.where(match, 1.0, 0.0)
+        weight = weight + jnp.where(match, route_ref[:, k : k + 1], 0.0)
+    earlier = lax.broadcasted_iota(jnp.int32, (routed, routed), 1) < lax.broadcasted_iota(
+        jnp.int32, (routed, routed), 0
+    )
+    slot_of = jnp.dot(
+        jnp.where(earlier, 1.0, 0.0).astype(bf16),
+        named.astype(bf16),
+        preferred_element_type=f32,
+    )
+    weight = jnp.where(slot_of == row.astype(f32), weight, 0.0)
+    for k in range(1, n_ep):
+        rows_land(k).wait_recv()
+    received = rows_in[...].reshape(width, columns)
+    result = residual_ref[...].astype(f32)
+    for _ in range(3):
+        piece = weight.astype(bf16)
+        result = result + jnp.dot(piece, received, preferred_element_type=f32)
+        weight = weight - piece.astype(f32)
+    input_grad_ref[...] = result.astype(bf16)
+
+    grad_in(1).wait_recv()
+    grad_in(2).wait_recv()
+    context_in(5).wait_recv()
+    chip_product(x_chip, False, False)
+    context_in(3).wait_recv()
+    context_out(7).start()
+    grad_in(3).wait_recv()
+    grad_in(4).wait_recv()
+    context_in(6).wait_recv()
+    context_in(4).wait_recv()
+    context_out(8).start()
+    chip_product(y_chip, False, False)
+    for i in (7, 8, 9):
+        grad_in(i).wait_recv()
+    context_in(7).wait_recv()
+    context_in(8).wait_recv()
+    chip_product(d_chip, False, True)
+
+    for i in range(9):
+        context_out(i).wait_send()
+    for i in range(10):
+        grad_out(i).wait_send()
+    for k in range(1, n_ep):
+        rows_move(k).wait_send()
+    for i in range(steps):
+        store(i).wait()
+
+
+def kernel_shards(
+    n_fsdp,
+    n_ep,
+    expert_ids,
+    route_weights,
+    residual_grad,
+    hidden_grad,
+    gate_pre,
+    up_pre,
+    gate_weight,
+    up_weight,
+    attn_context,
+    attn_grad,
+):
+    blocks, slots, hidden = hidden_grad.shape
+    columns = gate_weight.shape[1]
+    tokens, context_cols = attn_context.shape
+    cap = slots // n_ep
+    bf16, f32 = jnp.bfloat16, jnp.float32
+    vmem = pl.BlockSpec(memory_space=pltpu.VMEM)
+    anywhere = pl.BlockSpec(memory_space=pl.ANY)
+    dma = pltpu.SemaphoreType.DMA
+    steps = context_cols // 256
+    return pl.pallas_call(
+        functools.partial(kernel, n_ep),
+        out_shape=(
+            jax.ShapeDtypeStruct(residual_grad.shape, bf16),
+            jax.ShapeDtypeStruct((context_cols, columns), f32),
+        ),
+        in_specs=[vmem] * 3 + [anywhere] * 7,
+        out_specs=(vmem, anywhere),
+        scratch_shapes=[
+            pltpu.VMEM((SLOT_COUNT, slots, hidden), bf16),
+            pltpu.VMEM((SLOT_COUNT, slots, hidden), bf16),
+            pltpu.VMEM((SLOT_COUNT, slots, hidden), bf16),
+            pltpu.VMEM((SLOT_COUNT, columns, hidden), bf16),
+            pltpu.VMEM((SLOT_COUNT, columns, hidden), bf16),
+            pltpu.VMEM((slots, hidden), bf16),
+            pltpu.VMEM((slots, hidden), bf16),
+            pltpu.VMEM((slots, columns), f32),
+            pltpu.VMEM((n_ep, blocks // 2, cap, columns), bf16),
+            pltpu.VMEM((n_ep, blocks // 2, cap, columns), bf16),
+            pltpu.VMEM((n_fsdp, tokens, context_cols), bf16),
+            pltpu.VMEM((n_fsdp, tokens, columns), bf16),
+            pltpu.VMEM((context_cols, columns), f32),
+            dma((5, SLOT_COUNT)),
+            dma((2,)),
+            dma((steps,)),
+            dma((9,)),
+            dma((9,)),
+            dma((10,)),
+            dma((10,)),
+            dma((n_ep - 1,)),
+            dma((n_ep - 1,)),
+        ],
+        compiler_params=pltpu.CompilerParams(
+            collective_id=0, has_side_effects=True, vmem_limit_bytes=58 * 1024 * 1024
+        ),
+        cost_estimate=pl.CostEstimate(
+            flops=4 * blocks * slots * columns * hidden
+            + 2 * n_fsdp * tokens * context_cols * columns,
+            bytes_accessed=4 * blocks * columns * hidden + 6 * blocks * slots * hidden,
+            transcendentals=blocks * slots * hidden,
+        ),
+        name="expert_and_projection",
+    )(
+        expert_ids,
+        route_weights,
+        residual_grad,
+        hidden_grad,
+        gate_pre,
+        up_pre,
+        gate_weight,
+        up_weight,
+        attn_context,
+        attn_grad,
+    )
+
+
 def solution(mesh):
+    n_fsdp, n_ep = mesh.shape["fsdp"], mesh.shape["ep"]
+
+    def shards(*args):
+        weight, context = args[6], args[8]
+        fits = (
+            n_fsdp == 8
+            and n_ep == 4
+            and weight.shape[1] % 128 == 0
+            and context.shape[1] % 256 == 0
+            and context.shape[0] % (16 * n_ep) == 0
+            and args[3].shape[1] % (16 * n_ep) == 0
+        )
+        if fits:
+            return kernel_shards(n_fsdp, n_ep, *args)
+        return general_shards(*args)
+
     return jax.shard_map(
         shards,
         mesh=mesh,

time: 266 us -> 74.8 us (0.28)
  waiting for transfers between devices: 169 us -> 0 us
  Pallas kernels: 0 us -> 64.6 us
  matrix products: 62.5 us -> 0 us
  between operations: 14.1 us -> 0.64 us
  starting transfers between devices: 6.78 us -> 0 us
  local copies, waits for them, and re-layouts: 12.8 us -> 8.98 us
    reduce_scatter x1 -> x0, waiting for transfers between devices: 150 us -> none  [shards(): lax.psum_scatter(jnp.einsum('tj,ti->ji', attn_grad, attn_context, preferr...]
    pallas_call x0 -> x1, Pallas kernels: none -> 64.6 us  [kernel_shards(): pl.pallas_call(functools.partial(kernel, n_ep), out_shape=(jax.ShapeDtype...]
    dot_general x4 -> x0, matrix products: 62.5 us -> none  [the longest x1 25.9 us: shards(): jnp.einsum('brh,bdh->brd', gate_term, gate_weight, preferred_element_type...]
    all_to_all x1 -> x0, waiting for transfers between devices: 18.9 us -> none  [shards(): lax.all_to_all(rows_out, 'ep', split_axis=1, concat_axis=0, tiled=True)]
    all_to_all x1 -> x0, starting transfers between devices: 6.74 us -> none  [shards(): lax.all_to_all(rows_out, 'ep', split_axis=1, concat_axis=0, tiled=True)]
    unnamed x14 -> x4, local copies, waits for them, and re-layouts: 9.74 us -> 8.98 us
  transfers between devices with their start and end apart: 2 -> 0, of which waited for: 2 -> 0; matrix products, arithmetic and copies ran while one was open for 19% -> 0% of each run, Pallas kernels for 0% -> 0%
where the time goes in v1:
time: 74.8 us; the launch traced here: 74.2 us
  Pallas kernels  64.6 us (86%)
  local copies, waits for them, and re-layouts  8.98 us (12%)
    pallas_call x1, Pallas kernels, kernel_shards(): pl.pallas_call(functools.partial(kernel, n_ep), out_shape=(jax.ShapeDtype...  64.6 us
    unnamed x4, local copies, waits for them, and re-layouts  8.98 us

profile of v1, /device:TPU:0, one launch (start us, length us, event | category | flops | bytes accessed | tf_op | source)
XLA Modules:
  0.0 74.2 jit_solution(7706897805659547845)
XLA Ops:
  0.6 1.4 %copy.12.ids_ref = s32[32,4]{1,0:T(8,128)} copy(s32[32,4]{0,1:T(4,128)} %param.10) | data formatting | bytes 1024 | tf_op args[0]
  2.0 1.4 %copy.13.route_ref = f32[32,4]{1,0:T(8,128)} copy(f32[32,4]{0,1:T(4,128)} %param.11) | data formatting | bytes 1024 | tf_op args[1]
  3.4 64.6 %expert_and_projection.1 = (bf16[32,768]{1,0:T(8,128)(2,1)}, f32[1536,768]{1,0:T(8,128)}) custom-call(s32[32,4]{1,0:T(8,128)} %copy.12.ids_ref, f32[32,4]{1,0:T(8,128)} %copy.13.route_ref, bf16[32,768]{1,0:T(8,128)(2,1)} %residual_ref.1, bf16[8,64,2688]{2,1,0:T(8,128)(2,1)} %hidden_hbm.1, bf16[8,64,2688]{2,1,0:T(8,128)(2,1)} %gate_hbm.1, ...), custom_call_target="tpu_custom_call" | custom-call | flops 9059696640 | bytes 74317824 | tf_op jit(solution)/shard_map/expert_and_projection/pallas_call | solution.py:417
  68.0 1.4 %copy.16 = bf16[32,768]{1,0:T(8,128)(2,1)} copy(bf16[32,768]{1,0:T(8,128)(2,1)} %get-tuple-element.4) | data formatting | bytes 98304
  69.4 4.8 %copy.17 = f32[1536,768]{1,0:T(8,128)} copy(f32[1536,768]{1,0:T(8,128)} %get-tuple-element.5) | data formatting | bytes 9437184

commit v2 on v1

--- a/solution.py
+++ b/solution.py
@@ -70,7 +70,6 @@
     n_ep,
     ids_ref,
     route_ref,
-    residual_ref,
     hidden_hbm,
     gate_hbm,
     up_hbm,
@@ -78,8 +77,10 @@
     up_weight_hbm,
     context_hbm,
     grad_hbm,
-    input_grad_ref,
+    gathered_ref,
     proj_hbm,
+    far_context,
+    far_grad,
     hidden_buf,
     gate_buf,
     up_buf,
@@ -122,7 +123,7 @@
     x_same, x_other = at(y, 1 - x, core), at(y, 1 - x, 1 - core)
     y_same, y_other = at(1 - y, x, core), at(1 - y, x, 1 - core)
     d_same, d_other = at(1 - y, 1 - x, core), at(1 - y, 1 - x, 1 - core)
-    own_chip, x_chip, y_chip, d_chip = f // 2, x_same // 2, y_same // 2, d_same // 2
+    own_chip, x_chip, y_chip = f // 2, x_same // 2, y_same // 2
 
     sources = (gate_weight_hbm, up_weight_hbm, hidden_hbm, gate_hbm, up_hbm)
     buffers = (gate_weight_buf, up_weight_buf, hidden_buf, gate_buf, up_buf)
@@ -163,23 +164,23 @@
         (context_hbm, context_all.at[f], sib),
         (context_hbm, context_all.at[f], x_same),
         (context_hbm, context_all.at[f], y_same),
-        (context_all.at[x_same, first], context_all.at[x_same, first], y_same),
-        (context_all.at[y_same, second], context_all.at[y_same, second], x_same),
+        (context_all.at[x_same, first], far_context.at[core, first], y_same),
+        (context_all.at[y_same, second], far_context.at[core, second], x_same),
         (context_all.at[x_same], context_all.at[x_same], sib),
         (context_all.at[y_same], context_all.at[y_same], sib),
-        (context_all.at[d_same, first], context_all.at[d_same, first], sib),
-        (context_all.at[d_same, second], context_all.at[d_same, second], sib),
+        (far_context.at[core, first], far_context.at[core, first], sib),
+        (far_context.at[core, second], far_context.at[core, second], sib),
     )
     context_lands = (
         context_all.at[sib],
         context_all.at[x_same],
         context_all.at[y_same],
-        context_all.at[d_same, first],
-        context_all.at[d_same, second],
+        far_context.at[core, first],
+        far_context.at[core, second],
         context_all.at[x_other],
         context_all.at[y_other],
-        context_all.at[d_other, first],
-        context_all.at[d_other, second],
+        far_context.at[1 - core, first],
+        far_context.at[1 - core, second],
     )
 
     def context_out(i):
@@ -193,7 +194,6 @@
     def share(who):
         return pl.ds(pl.multiple_of(who * quarter, quarter), quarter)
 
-    pair = pl.ds(2 * d_chip, 2)
     grad_targets = (sib, x_same, x_other, y_same, y_other, d_same, d_other)
 
     def grad_out(i):
@@ -202,9 +202,9 @@
             src, dst = grad_hbm.at[:, grad_columns(to)], grad_all.at[f]
         elif i < 7:
             to = grad_targets[i]
-            src, dst = grad_hbm.at[share(z), grad_columns(to)], grad_all.at[f, share(z)]
+            src, dst = grad_hbm.at[share(z), grad_columns(to)], far_grad.at[core, share(z)]
         else:
-            src = dst = grad_all.at[pair, share(z)]
+            src = dst = far_grad.at[:, share(z)]
             return remote(src, dst, grad_send, grad_recv, i, (f, (z + i - 6) % n_ep))
         return remote(src, dst, grad_send, grad_recv, i, (to, z))
 
@@ -212,10 +212,11 @@
         if i < 5:
             land, to = grad_all.at[grad_targets[i]], (grad_targets[i], z)
         elif i < 7:
-            land, to = grad_all.at[grad_targets[i], share(z)], (grad_targets[i], z)
+            land = far_grad.at[core if i == 5 else 1 - core, share(z)]
+            to = (grad_targets[i], z)
         else:
             from_z = (z + n_ep - (i - 6)) % n_ep
-            land, to = grad_all.at[pair, share(from_z)], (f, from_z)
+            land, to = far_grad.at[:, share(from_z)], (f, from_z)
         return remote(land, land, grad_send, grad_recv, i, to)
 
     def rows_move(k):
@@ -279,10 +280,10 @@
             gate_term[:, cols] = (scaled * upper * (1.0 + gate * (1.0 - sig))).astype(bf16)
         dims = (((1,), (1,)), ((), ()))
         part = lax.dot_general(
-            gate_term[...], gate_weight_buf[slot], dims, preferred_element_type=f32
+            gate_weight_buf[slot], gate_term[...], dims, preferred_element_type=f32
         )
         part = part + lax.dot_general(
-            up_term[...], up_weight_buf[slot], dims, preferred_element_type=f32
+            up_weight_buf[slot], up_term[...], dims, preferred_element_type=f32
         )
 
         @pl.when(block % 2 == 0)
@@ -291,7 +292,7 @@
 
         @pl.when(block % 2 == 1)
         def _():
-            both = (half_rows[...] + part).astype(bf16)
+            both = (half_rows[...] + part).T.astype(bf16)
             for dest in range(n_ep):
                 rows_out[dest, block // 2] = both[dest * cap : (dest + 1) * cap]
 
@@ -334,34 +335,36 @@
     grad_in(0).wait_recv()
     chip_product(own_chip, True, False)
 
-    routed, top = ids_ref.shape
+    top, routed = ids_ref.shape
     width = n_ep * (blocks // 2) * cap
-    place = lax.broadcasted_iota(jnp.int32, (routed, width), 1)
+    place = lax.broadcasted_iota(jnp.int32, (width, routed), 0)
     expert, row = place // cap, place % cap
-    named = jnp.zeros((routed, width), f32)
-    weight = jnp.zeros((routed, width), f32)
+    named = jnp.zeros((width, routed), f32)
+    weight = jnp.zeros((width, routed), f32)
     for k in range(top):
-        match = ids_ref[:, k : k + 1] == expert
+        match = ids_ref[k : k + 1, :] == expert
         named = named + jnp.where(match, 1.0, 0.0)
-        weight = weight + jnp.where(match, route_ref[:, k : k + 1], 0.0)
-    earlier = lax.broadcasted_iota(jnp.int32, (routed, routed), 1) < lax.broadcasted_iota(
-        jnp.int32, (routed, routed), 0
+        weight = weight + jnp.where(match, route_ref[k : k + 1, :], 0.0)
+    earlier = lax.broadcasted_iota(jnp.int32, (routed, routed), 0) < lax.broadcasted_iota(
+        jnp.int32, (routed, routed), 1
     )
     slot_of = jnp.dot(
+        named.astype(bf16),
         jnp.where(earlier, 1.0, 0.0).astype(bf16),
-        named.astype(bf16),
         preferred_element_type=f32,
     )
     weight = jnp.where(slot_of == row.astype(f32), weight, 0.0)
     for k in range(1, n_ep):
         rows_land(k).wait_recv()
     received = rows_in[...].reshape(width, columns)
-    result = residual_ref[...].astype(f32)
+    gathered = jnp.zeros((routed, columns), f32)
     for _ in range(3):
         piece = weight.astype(bf16)
-        result = result + jnp.dot(piece, received, preferred_element_type=f32)
+        gathered = gathered + lax.dot_general(
+            piece, received, (((0,), (0,)), ((), ())), preferred_element_type=f32
+        )
         weight = weight - piece.astype(f32)
-    input_grad_ref[...] = result.astype(bf16)
+    gathered_ref[...] = gathered
 
     grad_in(1).wait_recv()
     grad_in(2).wait_recv()
@@ -374,12 +377,11 @@
     context_in(6).wait_recv()
     context_in(4).wait_recv()
     context_out(8).start()
-    chip_product(y_chip, False, False)
+    chip_product(y_chip, False, True)
     for i in (7, 8, 9):
         grad_in(i).wait_recv()
     context_in(7).wait_recv()
     context_in(8).wait_recv()
-    chip_product(d_chip, False, True)
 
     for i in range(9):
         context_out(i).wait_send()
@@ -414,14 +416,16 @@
     anywhere = pl.BlockSpec(memory_space=pl.ANY)
     dma = pltpu.SemaphoreType.DMA
     steps = context_cols // 256
-    return pl.pallas_call(
+    gathered, near, far_context, far_grad = pl.pallas_call(
         functools.partial(kernel, n_ep),
         out_shape=(
-            jax.ShapeDtypeStruct(residual_grad.shape, bf16),
+            jax.ShapeDtypeStruct(residual_grad.shape, f32),
             jax.ShapeDtypeStruct((context_cols, columns), f32),
+            jax.ShapeDtypeStruct((2, tokens, context_cols), bf16),
+            jax.ShapeDtypeStruct((2, tokens, columns), bf16),
         ),
-        in_specs=[vmem] * 3 + [anywhere] * 7,
-        out_specs=(vmem, anywhere),
+        in_specs=[vmem] * 2 + [anywhere] * 7,
+        out_specs=(vmem, anywhere, anywhere, anywhere),
         scratch_shapes=[
             pltpu.VMEM((SLOT_COUNT, slots, hidden), bf16),
             pltpu.VMEM((SLOT_COUNT, slots, hidden), bf16),
@@ -430,7 +434,7 @@
             pltpu.VMEM((SLOT_COUNT, columns, hidden), bf16),
             pltpu.VMEM((slots, hidden), bf16),
             pltpu.VMEM((slots, hidden), bf16),
-            pltpu.VMEM((slots, columns), f32),
+            pltpu.VMEM((columns, slots), f32),
             pltpu.VMEM((n_ep, blocks // 2, cap, columns), bf16),
             pltpu.VMEM((n_ep, blocks // 2, cap, columns), bf16),
             pltpu.VMEM((n_fsdp, tokens, context_cols), bf16),
@@ -457,9 +461,8 @@
         ),
         name="expert_and_projection",
     )(
-        expert_ids,
-        route_weights,
-        residual_grad,
+        expert_ids.T,
+        route_weights.T,
         hidden_grad,
         gate_pre,
         up_pre,
@@ -468,6 +471,14 @@
         attn_context,
         attn_grad,
     )
+    input_grad = (residual_grad.astype(f32) + gathered).astype(bf16)
+    far = lax.dot_general(
+        far_context.reshape(2 * tokens, context_cols),
+        far_grad.reshape(2 * tokens, columns),
+        (((0,), (0,)), ((), ())),
+        preferred_element_type=f32,
+    )
+    return input_grad, near + far
 
 
 def solution(mesh):

time: 74.8 us -> 71.7 us (0.959)
  local copies, waits for them, and re-layouts: 8.98 us -> 0.01 us
  matrix products: 0 us -> 6.68 us
  Pallas kernels: 64.6 us -> 61.8 us
  other arithmetic: 0 us -> 1.52 us
    unnamed x4 -> x2, local copies, waits for them, and re-layouts: 8.98 us -> 0.01 us
    dot_general x0 -> x1, matrix products: none -> 6.68 us  [kernel_shards(): lax.dot_general(far_context.reshape(2 * tokens, context_cols), far_grad.r...]
    pallas_call x1, Pallas kernels: 64.6 us -> 61.8 us  [kernel_shards(): pl.pallas_call(functools.partial(kernel, n_ep), out_shape=(jax.ShapeDtype...]
    convert_element_type x0 -> x1, other arithmetic: none -> 1.52 us  [kernel_shards(): input_grad = (residual_grad.astype(f32) + gathered).astype(bf16)]
where the time goes in v2:
time: 71.7 us; the launch traced here: 70.7 us
  Pallas kernels  61.8 us (86%)
  matrix products  6.68 us (9%)
  other arithmetic  1.52 us (2%)
    pallas_call x1, Pallas kernels, kernel_shards(): pl.pallas_call(functools.partial(kernel, n_ep), out_shape=(jax.ShapeDtype...  61.8 us
    dot_general x1, matrix products, kernel_shards(): lax.dot_general(far_context.reshape(2 * tokens, context_cols), far_grad.r...  6.68 us
    convert_element_type x1, other arithmetic, kernel_shards(): input_grad = (residual_grad.astype(f32) + gathered).astype(bf16)  1.52 us

profile of v2, /device:TPU:0, one launch (start us, length us, event | category | flops | bytes accessed | tf_op | source)
XLA Modules:
  0.0 70.7 jit_solution(14885873654148514990)
XLA Ops:
  0.6 0.0 copy-start
  0.6 61.8 %expert_and_projection.1 = (f32[32,768]{1,0:T(8,128)}, f32[1536,768]{1,0:T(8,128)}, bf16[2,256,1536]{2,1,0:T(8,128)(2,1)}, bf16[2,256,768]{2,1,0:T(8,128)(2,1)}) custom-call(s32[4,32]{1,0:T(4,128)} %bitcast.6, f32[4,32]{1,0:T(4,128)} %bitcast.7, bf16[8,64,2688]{2,1,0:T(8,128)(2,1)} %hidden_hbm.1, bf16[8,64,2688]{2,1,0:T(8,128)(2,1)} %gate_hbm.1, ...), custom_call_target="tpu_custom_call" | custom-call | flops 9059696640 | bytes 74317824 | tf_op jit(solution)/shard_map/expert_and_projection/pallas_call | solution.py:419
  62.5 0.0 copy-done
  62.5 1.5 %add_convert_fusion = bf16[32,768]{1,0:T(8,128)(2,1)} fusion(f32[32,768]{1,0:T(8,128)} %get-tuple-element.6, bf16[32,768]{1,0:T(8,128)(2,1)S(1)} %copy-done), kind=kLoop, calls=%fused_computation.1 | loop fusion | flops 73728 | bytes 196608 | tf_op jit(solution)/shard_map/convert_element_type | solution.py:474
  64.0 6.7 %bitcast_add_fusion = f32[1536,768]{1,0:T(8,128)} fusion(f32[1536,768]{1,0:T(8,128)} %get-tuple-element.7, bf16[2,256,1536]{2,1,0:T(8,128)(2,1)} %get-tuple-element.8, bf16[2,256,768]{2,1,0:T(8,128)(2,1)} %get-tuple-element.9), kind=kOutput, calls=%fused_computation | convolution fusion | flops 1209139200 | bytes 11796480 | tf_op jit(solution)/shard_map/dot_general | solution.py:475
Async XLA Ops:
  0.6 61.9 %copy-start = (bf16[32,768]{1,0:T(8,128)(2,1)S(1)}, bf16[32,768]{1,0:T(8,128)(2,1)}, u32[]{:S(2)}) copy-start(bf16[32,768]{1,0:T(8,128)(2,1)} %param.12) | copy-start | bytes 147460

commit v3 on v2

--- a/solution.py
+++ b/solution.py
@@ -234,10 +234,11 @@
         pl.semaphore_signal(barrier, inc=1, device_id=who, device_id_type=MESH)
     pl.semaphore_wait(barrier, len(peers))
 
+    for i in (5, 6):
+        grad_out(i).start()
     for i in (1, 2, 0):
         context_out(i).start()
-    for i in (5, 6, 0):
-        grad_out(i).start()
+    grad_out(0).start()
 
     chunk = hidden // 7 if hidden % (7 * 128) == 0 else hidden
 
@@ -252,6 +253,13 @@
         @pl.when(block == 2)
         def _():
             for i in (1, 3, 2, 4):
+                grad_out(i).start()
+
+        @pl.when(block == 3)
+        def _():
+            grad_in(5).wait_recv()
+            grad_in(6).wait_recv()
+            for i in (7, 8, 9):
                 grad_out(i).start()
 
         @pl.when(block == blocks - 2)
@@ -262,11 +270,6 @@
             context_in(2).wait_recv()
             context_out(4).start()
             context_out(6).start()
-            grad_in(5).wait_recv()
-            grad_in(6).wait_recv()
-            for i in (7, 8, 9):
-                grad_out(i).start()
-
         for copy in loads(block):
             copy.wait()
         for start in range(0, hidden, chunk):
@@ -391,6 +394,20 @@
         rows_move(k).wait_send()
     for i in range(steps):
         store(i).wait()
+
+
+def finish(residual_ref, gathered_ref, near_ref, context_ref, grad_ref, input_grad_ref, proj_ref):
+    @pl.when(pl.program_id(0) == 0)
+    def _():
+        result = residual_ref[...].astype(jnp.float32) + gathered_ref[...]
+        input_grad_ref[...] = result.astype(jnp.bfloat16)
+
+    pair, tokens, cols = context_ref.shape
+    left = context_ref[...].reshape(pair * tokens, cols)
+    right = grad_ref[...].reshape(pair * tokens, grad_ref.shape[2])
+    proj_ref[...] = near_ref[...] + lax.dot_general(
+        left, right, (((0,), (0,)), ((), ())), preferred_element_type=jnp.float32
+    )
 
 
 def kernel_shards(
@@ -471,14 +488,27 @@
         attn_context,
         attn_grad,
     )
-    input_grad = (residual_grad.astype(f32) + gathered).astype(bf16)
-    far = lax.dot_general(
-        far_context.reshape(2 * tokens, context_cols),
-        far_grad.reshape(2 * tokens, columns),
-        (((0,), (0,)), ((), ())),
-        preferred_element_type=f32,
-    )
-    return input_grad, near + far
+    return pl.pallas_call(
+        finish,
+        grid=(steps,),
+        out_shape=(
+            jax.ShapeDtypeStruct(residual_grad.shape, bf16),
+            jax.ShapeDtypeStruct((context_cols, columns), f32),
+        ),
+        in_specs=[
+            pl.BlockSpec(residual_grad.shape, lambda i: (0, 0)),
+            pl.BlockSpec(residual_grad.shape, lambda i: (0, 0)),
+            pl.BlockSpec((256, columns), lambda i: (i, 0)),
+            pl.BlockSpec((2, tokens, 256), lambda i: (0, 0, i)),
+            pl.BlockSpec((2, tokens, columns), lambda i: (0, 0, 0)),
+        ],
+        out_specs=(
+            pl.BlockSpec(residual_grad.shape, lambda i: (0, 0)),
+            pl.BlockSpec((256, columns), lambda i: (i, 0)),
+        ),
+        compiler_params=pltpu.CompilerParams(vmem_limit_bytes=60 * 1024 * 1024),
+        name="far_product",
+    )(residual_grad, gathered, near, far_context, far_grad)
 
 
 def solution(mesh):

time: 71.7 us -> 67.6 us (0.943)
  matrix products: 6.68 us -> 0 us
  Pallas kernels: 61.8 us -> 66.7 us
  other arithmetic: 1.52 us -> 0 us
    pallas_call x0 -> x1, Pallas kernels: none -> 7.65 us  [kernel_shards(): pl.pallas_call(finish, grid=(steps,), out_shape=(jax.ShapeDtypeStruct(res...]
    dot_general x1 -> x0, matrix products: 6.68 us -> none  [kernel_shards(): lax.dot_general(far_context.reshape(2 * tokens, context_cols), far_grad.r...]
    pallas_call x1, Pallas kernels: 61.8 us -> 59 us  [kernel_shards(): pl.pallas_call(functools.partial(kernel, n_ep), out_shape=(jax.ShapeDtype...]
    convert_element_type x1 -> x0, other arithmetic: 1.52 us -> none  [kernel_shards(): input_grad = (residual_grad.astype(f32) + gathered).astype(bf16)]
where the time goes in v3:
time: 67.6 us; the launch traced here: 67.3 us
  Pallas kernels  66.7 us (99%)
    pallas_call x1, Pallas kernels, kernel_shards(): pl.pallas_call(functools.partial(kernel, n_ep), out_shape=(jax.ShapeDtype...  59 us
    pallas_call x1, Pallas kernels, kernel_shards(): pl.pallas_call(finish, grid=(steps,), out_shape=(jax.ShapeDtypeStruct(res...  7.65 us

profile of v3, /device:TPU:0, one launch (start us, length us, event | category | flops | bytes accessed | tf_op | source)
XLA Modules:
  0.0 67.3 jit_solution(8029247204035062829)
XLA Ops:
  0.6 59.0 %expert_and_projection.1 = (f32[32,768]{1,0:T(8,128)}, f32[1536,768]{1,0:T(8,128)}, bf16[2,256,1536]{2,1,0:T(8,128)(2,1)}, bf16[2,256,768]{2,1,0:T(8,128)(2,1)}) custom-call(s32[4,32]{1,0:T(4,128)} %bitcast.2, f32[4,32]{1,0:T(4,128)} %bitcast.3, bf16[8,64,2688]{2,1,0:T(8,128)(2,1)} %hidden_hbm.1, bf16[8,64,2688]{2,1,0:T(8,128)(2,1)} %gate_hbm.1, ...), custom_call_target="tpu_custom_call" | custom-call | flops 9059696640 | bytes 74317824 | tf_op jit(solution)/shard_map/expert_and_projection/pallas_call | solution.py:436
  59.7 7.7 %far_product.1 = (bf16[32,768]{1,0:T(8,128)(2,1)}, f32[1536,768]{1,0:T(8,128)}) custom-call(bf16[32,768]{1,0:T(8,128)(2,1)} %residual_ref.1, f32[32,768]{1,0:T(8,128)} %get-tuple-element.6.gathered_ref, f32[1536,768]{1,0:T(8,128)} %get-tuple-element.7.near_ref, bf16[2,256,1536]{2,1,0:T(8,128)(2,1)} %get-tuple-element.8.context_ref, ...), custom_call_target="tpu_custom_call" | custom-call | tf_op jit(solution)/shard_map/far_product/pallas_call | solution.py:491
